TPU v7x, 32 devices: a whole 2x2x4 slice. The times are simulated.
32 devices in a mesh: dp: 16 (over z, y, x), ctx: 2 (over core).
Axes of the slice: x: 2, y: 2, z: 4, core: 2. Of those that a mesh axis runs over, the one named last changes fastest.
Arguments:
- queries: bfloat16 [4096, 4096], P(('dp', 'ctx')), may hold values from -150 to 150
- keys: bfloat16 [4096, 512], P(('dp', 'ctx')), may hold values from -4 to 4
- values: bfloat16 [4096, 512], P(('dp', 'ctx')), may hold values from -6 to 6
- lengths: int32 [32], replicated, may hold values from 1 to 512, 4096 in all
Outputs:
- attended: bfloat16 [4096, 4096], P(('dp', 'ctx'))
Inputs may be any that keep to these rules, and one draw needn't show every extreme that they name: lengths of the 32 documents sum to 4096; the largest is exactly 512.
All inputs are finite; a program needn't handle non-finite values.
Results may differ from a plain program's by a relative error of at most 0.0045.
Values may be sent and summed in bfloat16 or wider, within the bound.
No kernel may reach another device: no remote copies, remote signals or barrier semaphores. Data moves between devices by JAX's collectives and lax.ppermute only.
A program may use at most 128 MiB of HBM per device.

v0:
```python
import functools
import math

import jax
import jax.numpy as jnp
from jax import lax
from jax.experimental import pallas as pl
from jax.experimental.pallas import tpu as pltpu
from jax.sharding import PartitionSpec as P

HEAD_SIZE = 128
QUERY_HEADS = 32
KEY_VALUE_HEADS = 4
GROUP = QUERY_HEADS // KEY_VALUE_HEADS
HEADS_AT_ONCE = 4
EXCLUDED = -1e30
AXES = ("dp", "ctx")


FACTOR = math.log2(math.e) / math.sqrt(HEAD_SIZE)


def head_columns(i):
    return slice(i * HEAD_SIZE, (i + 1) * HEAD_SIZE)


def stacked(ref, heads):
    return jnp.concatenate([ref[:, head_columns(i)] for i in heads], axis=0)


def spread(ref, heads, rows, value):
    for n, i in enumerate(heads):
        ref[:, head_columns(i)] = value[n * rows : (n + 1) * rows].astype(ref.dtype)


def with_ones(value):
    return jnp.concatenate([value, jnp.ones(value.shape, value.dtype)], axis=1)


def scores_of(q, key, bias):
    scores = lax.dot_general(
        q, key, (((1,), (1,)), ((), ())), preferred_element_type=jnp.float32
    )
    return scores + jnp.concatenate([bias] * (q.shape[0] // bias.shape[0]), axis=0)


def weights_of(scores, top):
    return jnp.exp2((scores - top) * jnp.float32(FACTOR)).astype(jnp.bfloat16)


def normalised(summed, total):
    inverse = pl.reciprocal(total, approx=True)
    return summed * (inverse * (2.0 - total * inverse))


def chains():
    return [
        (range(h, h + HEADS_AT_ONCE), h // GROUP) for h in range(0, QUERY_HEADS, HEADS_AT_ONCE)
    ]


def in_turn(*stages):
    runs = chains()
    results = {}
    for turn in range(len(runs) + len(stages) - 1):
        for n, stage in enumerate(stages):
            i = turn - n
            if 0 <= i < len(runs):
                results[i] = stage(*runs[i], *results.pop(i, ()))


def pack_kernel(key_hbm, value_hbm, *refs):
    *outs, sems = refs
    rows = key_hbm.shape[0]
    copies = []
    for n, out in enumerate(outs):
        copies.append(pltpu.make_async_copy(key_hbm, out.at[:rows], sems.at[n, 0]))
        copies.append(pltpu.make_async_copy(value_hbm, out.at[rows:], sems.at[n, 1]))
    for copy in copies:
        copy.start()
    for copy in copies:
        copy.wait()


def pack(keys, values):
    rows, width = keys.shape
    packed = pltpu.VMEM((2 * rows, width), keys.dtype)
    return pl.pallas_call(
        pack_kernel,
        out_shape=(packed, packed),
        in_specs=[HBM, HBM],
        out_specs=(VMEM, VMEM),
        scratch_shapes=[pltpu.SemaphoreType.DMA((2, 2))],
    )(*in_hbm(keys, values))


def own_kernel(
    rounds, rows, own_ref, lengths_hbm, q_hbm,
    _, bias_ref, needed_ref, q_ref, top_ref, total_ref, sum_ref,
    own_bias_ref, lengths_ref, lengths_sem, q_sems,
):
    lengths_copy = pltpu.make_async_copy(lengths_hbm, lengths_ref, lengths_sem)
    lengths_copy.start()
    width = GROUP * HEAD_SIZE
    q_copies = []
    for g in range(KEY_VALUE_HEADS):
        at = slice(g * width, (g + 1) * width)
        q_copies.append(pltpu.make_async_copy(q_hbm.at[:, at], q_ref.at[:, at], q_sems.at[g]))
        q_copies[g].start()
    me = lax.axis_index("dp") * lax.axis_size("ctx") + lax.axis_index("ctx")
    first = me * rows
    query_pos = first + lax.broadcasted_iota(jnp.int32, (rows, rows), 0)
    lengths_copy.wait()

    def later(doc, carried):
        bound, start, first_start = carried
        start = jnp.where(query_pos >= bound, bound, start)
        first_start = jnp.where(first >= bound, bound, first_start)
        return bound + lengths_ref[doc], start, first_start

    zero = jnp.int32(0)
    _, start, first_start = lax.fori_loop(
        0,
        lengths_ref.shape[0],
        later,
        (zero, jnp.zeros((rows, rows), jnp.int32), zero),
        unroll=8,
    )
    needed_ref[0] = lax.div(first - first_start + (rows - 1), jnp.int32(rows))
    lane = lax.broadcasted_iota(jnp.int32, (rows, rows), 1)

    def bias_of(allowed):
        return jnp.where(allowed, jnp.float32(0.0), jnp.float32(EXCLUDED))

    key_pos = first + lane
    own_bias_ref[...] = bias_of((key_pos >= start) & (key_pos <= query_pos))
    for b in range(2 * rounds):
        key_pos = first - (b + 1) * rows + lane
        bias_ref[:, b * rows : (b + 1) * rows] = bias_of(key_pos >= start)

    def match(heads, g):
        if heads[0] % GROUP == 0:
            q_copies[g].wait()
        return (scores_of(stacked(q_ref, heads), own_ref[:rows, head_columns(g)], own_bias_ref[...]),)

    def weigh(heads, g, scores):
        top = jnp.max(scores, axis=1, keepdims=True)
        spread(top_ref, heads, rows, jnp.broadcast_to(top, scores.shape))
        return (weights_of(scores, top),)

    def gather(heads, g, weights):
        value = with_ones(own_ref[rows:, head_columns(g)])
        summed = jnp.dot(weights, value, preferred_element_type=jnp.float32)
        spread(sum_ref, heads, rows, summed[:, :HEAD_SIZE])
        spread(total_ref, heads, rows, summed[:, HEAD_SIZE:])

    in_turn(match, weigh, gather)


def in_vmem(*operands):
    return [pltpu.with_memory_space_constraint(x, pltpu.VMEM) for x in operands]


def in_hbm(*operands):
    return [pltpu.with_memory_space_constraint(x, pltpu.HBM) for x in operands]


SMEM = pl.BlockSpec(memory_space=pltpu.SMEM)
VMEM = pl.BlockSpec(memory_space=pltpu.VMEM)
HBM = pl.BlockSpec(memory_space=pltpu.HBM)


def own_part(lengths, queries, own, rounds):
    rows = queries.shape[0]
    partial = pltpu.VMEM(queries.shape, jnp.float32)
    return pl.pallas_call(
        functools.partial(own_kernel, rounds, rows),
        out_shape=(
            pltpu.VMEM(own.shape, own.dtype),
            pltpu.VMEM((rows, 2 * rounds * rows), jnp.float32),
            jax.ShapeDtypeStruct((1,), jnp.int32),
            pltpu.VMEM(queries.shape, queries.dtype),
            partial,
            partial,
            partial,
        ),
        in_specs=[VMEM, HBM, HBM],
        out_specs=(VMEM, VMEM, SMEM, VMEM, VMEM, VMEM, VMEM),
        input_output_aliases={0: 0},
        scratch_shapes=[
            pltpu.VMEM((rows, rows), jnp.float32),
            pltpu.SMEM(lengths.shape, jnp.int32),
            pltpu.SemaphoreType.DMA,
            pltpu.SemaphoreType.DMA((KEY_VALUE_HEADS,)),
        ],
        compiler_params=pltpu.CompilerParams(vmem_limit_bytes=32 * 1024 * 1024),
        cost_estimate=pl.CostEstimate(
            flops=4 * 10**9, bytes_accessed=16 * 10**6, transcendentals=rows * queries.size
        ),
    )(*in_vmem(own), *in_hbm(lengths, queries))


def behind_kernel(
    before, last, rows, needed_ref, bias_ref, q_ref, *refs
):
    width = GROUP * HEAD_SIZE
    beyond = needed_ref[0] - before
    *near_refs, further_ref, top_ref, total_ref, sum_ref = refs[: 5 if last else 6]
    refs = refs[5 if last else 6 :]
    if last:
        near_refs = (near_refs[0].at[:rows], near_refs[0].at[rows:])
    pairs = (near_refs, (further_ref.at[:rows], further_ref.at[rows:]))
    if last:
        out_hbm, out_ref, out_sems = refs

        def out_copy(g):
            at = slice(g * width, (g + 1) * width)
            return pltpu.make_async_copy(out_ref.at[:, at], out_hbm.at[:, at], out_sems.at[g])

    else:
        _, new_top_ref, new_total_ref, new_sum_ref = refs

    def finish(heads, g, summed, total):
        if last:
            spread(out_ref, heads, rows, normalised(summed, total))
            if heads[-1] % GROUP == GROUP - 1:
                out_copy(g).start()
        else:
            spread(new_sum_ref, heads, rows, summed)
            spread(new_total_ref, heads, rows, total)

    def attend(count):
        def match(heads, g):
            key = jnp.concatenate([key[:, head_columns(g)] for key, _ in pairs[:count]], axis=0)
            bias = bias_ref[:, before * rows : (before + count) * rows]
            return (scores_of(stacked(q_ref, heads), key, bias),)

        def weigh(heads, g, scores):
            old_top = stacked(top_ref, heads)
            top = jnp.maximum(old_top, jnp.max(scores, axis=1, keepdims=True))
            fade = jnp.exp2((old_top - top) * jnp.float32(FACTOR))
            if not last:
                spread(new_top_ref, heads, rows, top)
            return weights_of(scores, jnp.concatenate([top] * count, axis=1)), fade

        def gather(heads, g, weights, fade):
            value = jnp.concatenate([value[:, head_columns(g)] for _, value in pairs[:count]], axis=0)
            more = jnp.dot(weights, with_ones(value), preferred_element_type=jnp.float32)
            summed = stacked(sum_ref, heads) * fade + more[:, :HEAD_SIZE]
            total = stacked(total_ref, heads) * fade + more[:, HEAD_SIZE:]
            finish(heads, g, summed, total)

        in_turn(match, weigh, gather)

    @pl.when(beyond > 1)
    def _():
        attend(2)

    @pl.when(beyond == 1)
    def _():
        attend(1)

    if last:
        @pl.when(beyond < 1)
        def _():
            in_turn(
                lambda heads, g: finish(heads, g, stacked(sum_ref, heads), stacked(total_ref, heads))
            )

        for g in range(KEY_VALUE_HEADS):
            out_copy(g).wait()


def behind_part(before, last, needed, bias, queries, halves, further, parts):
    rows = queries.shape[0]
    area = rows * rows * 2 * QUERY_HEADS
    operands = in_vmem(bias, queries, *halves, further, *parts)
    if last:
        out_shape = jax.ShapeDtypeStruct(queries.shape, queries.dtype)
        out_specs = HBM
        scratch = [
            pltpu.VMEM(queries.shape, queries.dtype),
            pltpu.SemaphoreType.DMA((KEY_VALUE_HEADS,)),
        ]
        aliases = {}
    else:
        kept = (further, *parts)
        out_shape = tuple(pltpu.VMEM(part.shape, part.dtype) for part in kept)
        out_specs = (VMEM,) * len(kept)
        scratch = []
        aliases = {5 + n: n for n in range(len(kept))}
    return pl.pallas_call(
        functools.partial(behind_kernel, before, last, rows),
        out_shape=out_shape,
        in_specs=[SMEM] + [VMEM] * len(operands),
        out_specs=out_specs,
        scratch_shapes=scratch,
        input_output_aliases=aliases,
        compiler_params=pltpu.CompilerParams(vmem_limit_bytes=32 * 1024 * 1024),
        cost_estimate=pl.CostEstimate(
            flops=4 * area, bytes_accessed=queries.size, transcendentals=0
        ),
    )(needed, *operands)


def per_device(queries, keys, values, lengths):
    count = lax.axis_size("dp") * lax.axis_size("ctx")
    rounds = lax.axis_size("ctx")

    def from_behind(block, r):
        by = 2 * (r + 1)
        return lax.ppermute(block, AXES, [(i, i + by) for i in range(count - by)])

    packed, own = pack(keys, values)
    fetched = [from_behind(packed, 0)]
    own, bias, needed, queries, *parts = own_part(lengths, queries, own, rounds)
    fetched += [from_behind(own, r) for r in range(1, rounds)]
    swap = [(i, i ^ 1) for i in range(count)]
    is_odd = lax.rem(lax.axis_index("ctx"), 2) == 1
    nearer = own
    for r, further in enumerate(fetched):
        last = r == rounds - 1
        cuts = 1 if last else 2
        halves = []
        for old, new in zip(jnp.split(nearer, cuts), jnp.split(further, cuts)):
            halves.append(lax.ppermute(jnp.where(is_odd, new, old), AXES, swap))
        result = behind_part(2 * r, last, needed, bias, queries, halves, further, parts)
        if not last:
            nearer, *parts = result
    return result


def solution(mesh):
    in_specs = (P(AXES, None), P(AXES, None), P(AXES, None), P())
    return jax.shard_map(
        per_device, mesh=mesh, in_specs=in_specs, out_specs=P(AXES, None), check_vma=False
    )
```

profile of v0, /device:TPU:0, one launch (start us, length us, event | category | flops | bytes accessed | tf_op | source)
XLA Modules:
  0.0 33.9 jit_solution(7800886592004395847)
XLA Ops:
  0.0 1.9 %shard_map.46 = (bf16[256,512]{1,0:T(8,128)(2,1)}, bf16[256,512]{1,0:T(8,128)(2,1)}) custom-call(bf16[128,512]{1,0:T(8,128)(2,1)} %key_hbm.1, bf16[128,512]{1,0:T(8,128)(2,1)} %value_hbm.1), custom_call_target="tpu_custom_call" | custom-call | tf_op jit(solution)/shard_map/pallas_call | solution.py:88
  1.9 4.9 %collective-permute-start.1 = (bf16[256,512]{1,0:T(8,128)(2,1)}, bf16[256,512]{1,0:T(8,128)(2,1)S(1)}, u32[]{:S(2)}, u32[]{:S(2)}) collective-permute-start(bf16[256,512]{1,0:T(8,128)(2,1)} %get-tuple-element.23), channel_id=1, source_target_pairs={{0,2},{1,3},{2,4},{3,5},{4,6},{5,7},{6,8},{7,9},{8,10},{9,11},{10,... | collective-permute-start | bytes 786440 | tf_op jit(solution)/shard_map/ppermute | solution.py:312
  6.8 4.0 %shard_map.47 = (bf16[256,512]{1,0:T(8,128)(2,1)}, f32[128,512]{1,0:T(8,128)S(1)}, s32[1]{0:T(128)}, bf16[128,4096]{1,0:T(8,128)(2,1)S(1)}, f32[128,4096]{1,0:T(...) custom-call(bf16[256,512]{1,0:T(8,128)(2,1)} %get-tuple-element.18.own_ref, ...), custom_call_target="tpu_custom_call", output_to_operand_aliasing={{0}: (0, {})} | custom-call | flops 4000000000 | bytes 16000000 | tf_op jit(solution)/shard_map/pallas_call | solution.py:176
  10.8 0.0 copy-start
  10.8 1.3 %copy-done = f32[128,4096]{1,0:T(8,128)} copy-done((f32[128,4096]{1,0:T(8,128)}, f32[128,4096]{1,0:T(8,128)S(1)}, u32[]{:S(2)}) %copy-start) | copy-done | bytes 2097176
  12.2 0.0 copy-start.2
  12.2 1.3 %copy-done.2 = f32[128,4096]{1,0:T(8,128)} copy-done((f32[128,4096]{1,0:T(8,128)}, f32[128,4096]{1,0:T(8,128)S(1)}, u32[]{:S(2)}) %copy-start.2) | copy-done | bytes 2097176
  13.5 0.0 copy-start.4
  13.5 0.7 %copy-done.4 = f32[128,512]{1,0:T(8,128)} copy-done((f32[128,512]{1,0:T(8,128)}, f32[128,512]{1,0:T(8,128)S(1)}, u32[]{:S(2)}) %copy-start.4) | copy-done | bytes 262168
  14.2 4.1 %collective-permute-start = (bf16[256,512]{1,0:T(8,128)(2,1)}, bf16[256,512]{1,0:T(8,128)(2,1)}, u32[]{:S(2)}, u32[]{:S(2)}) collective-permute-start(bf16[256,512]{1,0:T(8,128)(2,1)} %get-tuple-element.22), channel_id=1, source_target_pairs={{0,4},{1,5},{2,6},{3,7},{4,8},{5,9},{6,10},{7,11},{8,12},{9,13},{1... | collective-permute-start | bytes 786440 | tf_op jit(solution)/shard_map/ppermute | solution.py:312
  18.3 0.0 collective-permute-done.1.refs_2_
  18.3 1.0 %slice_select_fusion = (bf16[128,512]{1,0:T(8,128)(2,1)S(1)}, bf16[128,512]{1,0:T(8,128)(2,1)S(1)}) fusion(bf16[256,512]{1,0:T(8,128)(2,1)S(1)} %collective-permute-done.1.refs_2_, bf16[256,512]{1,0:T(8,128)(2,1)} %get-tuple-element.22, pred[]{:T(512)S(6)} %eq.3), kind=kLoop, calls=%fused_computation.1 | loop fusion | flops 131072 | bytes 786433 | tf_op jit(solution)/shard_map/jit(_where)/select_n | solution.py:326
  19.3 0.1 collective-permute-start.3
  19.4 0.5 %collective-permute-start.2 = (bf16[128,512]{1,0:T(8,128)(2,1)S(1)}, bf16[128,512]{1,0:T(8,128)(2,1)S(1)}, u32[]{:S(2)}, u32[]{:S(2)}) collective-permute-start(bf16[128,512]{1,0:T(8,128)(2,1)S(1)} %get-tuple-element.32), channel_id=1, source_target_pairs={{0,1},{1,0},{2,3},{3,2},{4,5},{5,4},{6,7},{7,6},{8,9},{9,8},{10,11... | collective-permute-start | bytes 393224 | tf_op jit(solution)/shard_map/ppermute | solution.py:326
  19.9 0.8 %collective-permute-done.3.refs_1_ = bf16[128,512]{1,0:T(8,128)(2,1)S(1)} collective-permute-done((bf16[128,512]{1,0:T(8,128)(2,1)S(1)}, bf16[128,512]{1,0:T(8,128)(2,1)S(1)}, u32[]{:S(2)}, u32[]{:S(2)}) %collective-permute-start.3) | collective-permute-done | bytes 131104 | tf_op jit(solution)/shard_map/ppermute | solution.py:326
  20.7 0.2 collective-permute-done.2.refs_0_
  20.9 0.0 copy-start.1
  20.9 1.6 %copy-done.1 = f32[128,4096]{1,0:T(8,128)S(1)} copy-done((f32[128,4096]{1,0:T(8,128)S(1)}, f32[128,4096]{1,0:T(8,128)}, u32[]{:S(2)}) %copy-start.1) | copy-done | bytes 2097176
  22.5 0.0 copy-start.3
  22.5 1.6 %copy-done.3 = f32[128,4096]{1,0:T(8,128)S(1)} copy-done((f32[128,4096]{1,0:T(8,128)S(1)}, f32[128,4096]{1,0:T(8,128)}, u32[]{:S(2)}) %copy-start.3) | copy-done | bytes 2097176
  24.1 0.0 copy-start.5
  24.1 0.9 %copy-done.5 = f32[128,512]{1,0:T(8,128)S(1)} copy-done((f32[128,512]{1,0:T(8,128)S(1)}, f32[128,512]{1,0:T(8,128)}, u32[]{:S(2)}) %copy-start.5) | copy-done | bytes 262168
  25.1 0.6 %shard_map.48 = (bf16[256,512]{1,0:T(8,128)(2,1)S(1)}, f32[128,4096]{1,0:T(8,128)S(1)}, f32[128,4096]{1,0:T(8,128)S(1)}, f32[128,4096]{1,0:T(8,128)S(1)}) custom-call(s32[1]{0:T(128)} %get-tuple-element.19.needed_ref, f32[128,512]{1,0:T(8,128)S(1)} %copy-done.5, ...), custom_call_target="tpu_custom_call", output_to_operand_aliasing={{0}: (5, {}), {1}: (6, {}), {2}: (7, {}), {3}: (8, {})} | custom-call | flops 4194304 | bytes 524288 | tf_op jit(solution)/shard_map/pallas_call | solution.py:292
  25.7 0.0 collective-permute-done.refs_1_
  25.8 4.1 %collective-permute-start.4 = (bf16[256,512]{1,0:T(8,128)(2,1)S(1)}, bf16[256,512]{1,0:T(8,128)(2,1)S(1)}, u32[]{:S(2)}, u32[]{:S(2)}) collective-permute-start(bf16[256,512]{1,0:T(8,128)(2,1)S(1)} %broadcast_select_fusion), channel_id=1, source_target_pairs={{0,1},{1,0},{2,3},{3,2},{4,5},{5,4},{6,7},{7,6},{8,9},{9,8},{10,11... | collective-permute-start | bytes 786440 | tf_op jit(solution)/shard_map/ppermute | solution.py:326
  29.9 1.2 %collective-permute-done.4.refs_0_ = bf16[256,512]{1,0:T(8,128)(2,1)S(1)} collective-permute-done((bf16[256,512]{1,0:T(8,128)(2,1)S(1)}, bf16[256,512]{1,0:T(8,128)(2,1)S(1)}, u32[]{:S(2)}, u32[]{:S(2)}) %collective-permute-start.4) | collective-permute-done | bytes 262176 | tf_op jit(solution)/shard_map/ppermute | solution.py:326
  31.1 2.8 %shard_map.49 = bf16[128,4096]{1,0:T(8,128)(2,1)} custom-call(s32[1]{0:T(128)} %get-tuple-element.19.needed_ref, f32[128,512]{1,0:T(8,128)S(1)} %copy-done.5, bf16[128,4096]{1,0:T(8,128)(2,1)S(1)} %get-tuple-element.21.q_ref, bf16[256,512]{1,0:T(8,128)(2,1)S(1)} %collective-permute-done.4.refs_0_, bf16[256,512]{1,0:T(8,128)(2,1)} %collective-permute-done.refs_1_, ...), custom_call_target="tpu_custom_call" | custom-call | flops 4194304 | bytes 524288 | tf_op jit(solution)/shard_map/pallas_call | solution.py:292
  (1 shorter events, 0.0 us)
Async XLA Ops:
  1.9 16.4 %collective-permute-start.1 = (bf16[256,512]{1,0:T(8,128)(2,1)}, bf16[256,512]{1,0:T(8,128)(2,1)S(1)}, u32[]{:S(2)}, u32[]{:S(2)}) collective-permute-start(bf16[256,512]{1,0:T(8,128)(2,1)} %get-tuple-element.23), channel_id=1, source_target_pairs={{0,2},{1,3},{2,4},{3,5},{4,6},{5,7},{6,8},{7,9},{8,10},{9,11},{10,... | collective-permute-start | bytes 786440 | tf_op jit(solution)/shard_map/ppermute | solution.py:312
  10.8 1.3 %copy-start = (f32[128,4096]{1,0:T(8,128)}, f32[128,4096]{1,0:T(8,128)S(1)}, u32[]{:S(2)}) copy-start(f32[128,4096]{1,0:T(8,128)S(1)} %get-tuple-element.25.refs_4_) | copy-start | bytes 6291460
  12.2 1.3 %copy-start.2 = (f32[128,4096]{1,0:T(8,128)}, f32[128,4096]{1,0:T(8,128)S(1)}, u32[]{:S(2)}) copy-start(f32[128,4096]{1,0:T(8,128)S(1)} %get-tuple-element.26.refs_5_) | copy-start | bytes 6291460
  13.5 0.7 %copy-start.4 = (f32[128,512]{1,0:T(8,128)}, f32[128,512]{1,0:T(8,128)S(1)}, u32[]{:S(2)}) copy-start(f32[128,512]{1,0:T(8,128)S(1)} %get-tuple-element.20.bias_ref) | copy-start | bytes 786436
  14.2 11.5 %collective-permute-start = (bf16[256,512]{1,0:T(8,128)(2,1)}, bf16[256,512]{1,0:T(8,128)(2,1)}, u32[]{:S(2)}, u32[]{:S(2)}) collective-permute-start(bf16[256,512]{1,0:T(8,128)(2,1)} %get-tuple-element.22), channel_id=1, source_target_pairs={{0,4},{1,5},{2,6},{3,7},{4,8},{5,9},{6,10},{7,11},{8,12},{9,13},{1... | collective-permute-start | bytes 786440 | tf_op jit(solution)/shard_map/ppermute | solution.py:312
  19.3 1.4 %collective-permute-start.3 = (bf16[128,512]{1,0:T(8,128)(2,1)S(1)}, bf16[128,512]{1,0:T(8,128)(2,1)S(1)}, u32[]{:S(2)}, u32[]{:S(2)}) collective-permute-start(bf16[128,512]{1,0:T(8,128)(2,1)S(1)} %get-tuple-element.31), channel_id=1, source_target_pairs={{0,1},{1,0},{2,3},{3,2},{4,5},{5,4},{6,7},{7,6},{8,9},{9,8},{10,11... | collective-permute-start | bytes 393224 | tf_op jit(solution)/shard_map/ppermute | solution.py:326
  19.4 1.5 %collective-permute-start.2 = (bf16[128,512]{1,0:T(8,128)(2,1)S(1)}, bf16[128,512]{1,0:T(8,128)(2,1)S(1)}, u32[]{:S(2)}, u32[]{:S(2)}) collective-permute-start(bf16[128,512]{1,0:T(8,128)(2,1)S(1)} %get-tuple-element.32), channel_id=1, source_target_pairs={{0,1},{1,0},{2,3},{3,2},{4,5},{5,4},{6,7},{7,6},{8,9},{9,8},{10,11... | collective-permute-start | bytes 393224 | tf_op jit(solution)/shard_map/ppermute | solution.py:326
  20.9 1.6 %copy-start.1 = (f32[128,4096]{1,0:T(8,128)S(1)}, f32[128,4096]{1,0:T(8,128)}, u32[]{:S(2)}) copy-start(f32[128,4096]{1,0:T(8,128)} %copy-done) | copy-start | bytes 6291460
  22.5 1.6 %copy-start.3 = (f32[128,4096]{1,0:T(8,128)S(1)}, f32[128,4096]{1,0:T(8,128)}, u32[]{:S(2)}) copy-start(f32[128,4096]{1,0:T(8,128)} %copy-done.2) | copy-start | bytes 6291460
  24.1 0.9 %copy-start.5 = (f32[128,512]{1,0:T(8,128)S(1)}, f32[128,512]{1,0:T(8,128)}, u32[]{:S(2)}) copy-start(f32[128,512]{1,0:T(8,128)} %copy-done.4) | copy-start | bytes 786436
  25.8 5.3 %collective-permute-start.4 = (bf16[256,512]{1,0:T(8,128)(2,1)S(1)}, bf16[256,512]{1,0:T(8,128)(2,1)S(1)}, u32[]{:S(2)}, u32[]{:S(2)}) collective-permute-start(bf16[256,512]{1,0:T(8,128)(2,1)S(1)} %broadcast_select_fusion), channel_id=1, source_target_pairs={{0,1},{1,0},{2,3},{3,2},{4,5},{5,4},{6,7},{7,6},{8,9},{9,8},{10,11... | collective-permute-start | bytes 786440 | tf_op jit(solution)/shard_map/ppermute | solution.py:326
where the time goes:
time: 34.3 us; the launch traced here: 33.9 us
  starting transfers between devices  13.7 us (40%)
  Pallas kernels  9.41 us (27%)
  local copies, waits for them, and re-layouts  7.5 us (22%)
  waiting for transfers between devices  2.19 us (6%)
  other arithmetic  1.04 us (3%)
    ppermute x2, starting transfers between devices, from_behind(): return lax.ppermute(block, AXES, [(i, i + by) for i in range(count - by)])  8.98 us
    unnamed x12, local copies, waits for them, and re-layouts  7.5 us
    ppermute x3, starting transfers between devices, per_device(): halves.append(lax.ppermute(jnp.where(is_odd, new, old), AXES, swap))  4.7 us
    pallas_call x1, Pallas kernels, own_part(): pl.pallas_call(functools.partial(own_kernel, rounds, rows), out_shape=(pl...  4 us
    pallas_call x2, Pallas kernels, behind_part(): pl.pallas_call(functools.partial(behind_kernel, before, last, rows), out_...  3.48 us
    ppermute x3, waiting for transfers between devices, per_device(): halves.append(lax.ppermute(jnp.where(is_odd, new, old), AXES, swap))  2.19 us
    pallas_call x1, Pallas kernels, pack(): pl.pallas_call(pack_kernel, out_shape=(packed, packed), in_specs=[HBM, HB...  1.93 us
    select_n x2, other arithmetic, per_device(): halves.append(lax.ppermute(jnp.where(is_odd, new, old), AXES, swap))  1.04 us
  transfers between devices with their start and end apart: 5, of which 3 were waited for; matrix products, arithmetic and copies ran while one was open for 3% of the time, Pallas kernels for 14%

commit v1 on v0

--- a/solution.py
+++ b/solution.py
@@ -193,7 +193,7 @@
             pltpu.SemaphoreType.DMA,
             pltpu.SemaphoreType.DMA((KEY_VALUE_HEADS,)),
         ],
-        compiler_params=pltpu.CompilerParams(vmem_limit_bytes=32 * 1024 * 1024),
+        compiler_params=pltpu.CompilerParams(vmem_limit_bytes=10 * 1024 * 1024),
         cost_estimate=pl.CostEstimate(
             flops=4 * 10**9, bytes_accessed=16 * 10**6, transcendentals=rows * queries.size
         ),
@@ -296,7 +296,7 @@
         out_specs=out_specs,
         scratch_shapes=scratch,
         input_output_aliases=aliases,
-        compiler_params=pltpu.CompilerParams(vmem_limit_bytes=32 * 1024 * 1024),
+        compiler_params=pltpu.CompilerParams(vmem_limit_bytes=10 * 1024 * 1024),
         cost_estimate=pl.CostEstimate(
             flops=4 * area, bytes_accessed=queries.size, transcendentals=0
         ),

time: 34.3 us -> 37.6 us (1.096)
  local copies, waits for them, and re-layouts: 7.5 us -> 10.4 us
    unnamed x12 -> x18, local copies, waits for them, and re-layouts: 7.5 us -> 10.4 us
  transfers between devices with their start and end apart: 5 -> 5, of which waited for: 3 -> 3; matrix products, arithmetic and copies ran while one was open for 3% -> 3% of each run, Pallas kernels for 14% -> 13%
where the time goes in v1:
time: 37.6 us; the launch traced here: 36.9 us
  starting transfers between devices  13.7 us (36%)
  local copies, waits for them, and re-layouts  10.4 us (28%)
  Pallas kernels  9.54 us (25%)
  waiting for transfers between devices  2.19 us (6%)
  other arithmetic  1.03 us (3%)
    unnamed x18, local copies, waits for them, and re-layouts  10.4 us
    ppermute x2, starting transfers between devices, from_behind(): return lax.ppermute(block, AXES, [(i, i + by) for i in range(count - by)])  8.97 us
    ppermute x3, starting transfers between devices, per_device(): halves.append(lax.ppermute(jnp.where(is_odd, new, old), AXES, swap))  4.7 us
    pallas_call x1, Pallas kernels, own_part(): pl.pallas_call(functools.partial(own_kernel, rounds, rows), out_shape=(pl...  3.98 us
    pallas_call x2, Pallas kernels, behind_part(): pl.pallas_call(functools.partial(behind_kernel, before, last, rows), out_...  3.64 us
    ppermute x3, waiting for transfers between devices, per_device(): halves.append(lax.ppermute(jnp.where(is_odd, new, old), AXES, swap))  2.19 us
    pallas_call x1, Pallas kernels, pack(): pl.pallas_call(pack_kernel, out_shape=(packed, packed), in_specs=[HBM, HB...  1.92 us
    select_n x2, other arithmetic, per_device(): halves.append(lax.ppermute(jnp.where(is_odd, new, old), AXES, swap))  1.03 us
  transfers between devices with their start and end apart: 5, of which 3 were waited for; matrix products, arithmetic and copies ran while one was open for 3% of the time, Pallas kernels for 13%

profile of v1, /device:TPU:0, one launch (start us, length us, event | category | flops | bytes accessed | tf_op | source)
XLA Modules:
  0.0 36.9 jit_solution(933233811999617184)
XLA Ops:
  0.0 1.9 %shard_map.46 = (bf16[256,512]{1,0:T(8,128)(2,1)}, bf16[256,512]{1,0:T(8,128)(2,1)}) custom-call(bf16[128,512]{1,0:T(8,128)(2,1)} %key_hbm.1, bf16[128,512]{1,0:T(8,128)(2,1)} %value_hbm.1), custom_call_target="tpu_custom_call" | custom-call | tf_op jit(solution)/shard_map/pallas_call | solution.py:88
  1.9 4.9 %collective-permute-start.1 = (bf16[256,512]{1,0:T(8,128)(2,1)}, bf16[256,512]{1,0:T(8,128)(2,1)S(1)}, u32[]{:S(2)}, u32[]{:S(2)}) collective-permute-start(bf16[256,512]{1,0:T(8,128)(2,1)} %get-tuple-element.23), channel_id=1, source_target_pairs={{0,2},{1,3},{2,4},{3,5},{4,6},{5,7},{6,8},{7,9},{8,10},{9,11},{10,... | collective-permute-start | bytes 786440 | tf_op jit(solution)/shard_map/ppermute | solution.py:312
  6.8 4.0 %shard_map.47 = (bf16[256,512]{1,0:T(8,128)(2,1)}, f32[128,512]{1,0:T(8,128)S(1)}, s32[1]{0:T(128)}, bf16[128,4096]{1,0:T(8,128)(2,1)S(1)}, f32[128,4096]{1,0:T(...) custom-call(bf16[256,512]{1,0:T(8,128)(2,1)} %get-tuple-element.18.own_ref, ...), custom_call_target="tpu_custom_call", output_to_operand_aliasing={{0}: (0, {})} | custom-call | flops 4000000000 | bytes 16000000 | tf_op jit(solution)/shard_map/pallas_call | solution.py:176
  10.8 0.0 copy-start
  10.8 1.3 %copy-done = f32[128,4096]{1,0:T(8,128)} copy-done((f32[128,4096]{1,0:T(8,128)}, f32[128,4096]{1,0:T(8,128)S(1)}, u32[]{:S(2)}) %copy-start) | copy-done | bytes 2097176
  12.1 0.0 copy-start.4
  12.1 1.3 %copy-done.4 = f32[128,4096]{1,0:T(8,128)} copy-done((f32[128,4096]{1,0:T(8,128)}, f32[128,4096]{1,0:T(8,128)S(1)}, u32[]{:S(2)}) %copy-start.4) | copy-done | bytes 2097176
  13.5 0.0 copy-start.6
  13.5 0.7 %copy-done.6 = f32[128,512]{1,0:T(8,128)} copy-done((f32[128,512]{1,0:T(8,128)}, f32[128,512]{1,0:T(8,128)S(1)}, u32[]{:S(2)}) %copy-start.6) | copy-done | bytes 262168
  14.2 4.1 %collective-permute-start = (bf16[256,512]{1,0:T(8,128)(2,1)}, bf16[256,512]{1,0:T(8,128)(2,1)}, u32[]{:S(2)}, u32[]{:S(2)}) collective-permute-start(bf16[256,512]{1,0:T(8,128)(2,1)} %get-tuple-element.22), channel_id=1, source_target_pairs={{0,4},{1,5},{2,6},{3,7},{4,8},{5,9},{6,10},{7,11},{8,12},{9,13},{1... | collective-permute-start | bytes 786440 | tf_op jit(solution)/shard_map/ppermute | solution.py:312
  18.3 0.0 collective-permute-done.1.refs_2_
  18.3 1.0 %slice_select_fusion = (bf16[128,512]{1,0:T(8,128)(2,1)S(1)}, bf16[128,512]{1,0:T(8,128)(2,1)S(1)}) fusion(bf16[256,512]{1,0:T(8,128)(2,1)S(1)} %collective-permute-done.1.refs_2_, bf16[256,512]{1,0:T(8,128)(2,1)} %get-tuple-element.22, pred[]{:T(512)S(6)} %eq.3), kind=kLoop, calls=%fused_computation.1 | loop fusion | flops 131072 | bytes 786433 | tf_op jit(solution)/shard_map/jit(_where)/select_n | solution.py:326
  19.3 0.1 collective-permute-start.3
  19.3 0.5 %collective-permute-start.2 = (bf16[128,512]{1,0:T(8,128)(2,1)S(1)}, bf16[128,512]{1,0:T(8,128)(2,1)S(1)}, u32[]{:S(2)}, u32[]{:S(2)}) collective-permute-start(bf16[128,512]{1,0:T(8,128)(2,1)S(1)} %get-tuple-element.32), channel_id=1, source_target_pairs={{0,1},{1,0},{2,3},{3,2},{4,5},{5,4},{6,7},{7,6},{8,9},{9,8},{10,11... | collective-permute-start | bytes 393224 | tf_op jit(solution)/shard_map/ppermute | solution.py:326
  19.8 0.8 %collective-permute-done.3.refs_1_ = bf16[128,512]{1,0:T(8,128)(2,1)S(1)} collective-permute-done((bf16[128,512]{1,0:T(8,128)(2,1)S(1)}, bf16[128,512]{1,0:T(8,128)(2,1)S(1)}, u32[]{:S(2)}, u32[]{:S(2)}) %collective-permute-start.3) | collective-permute-done | bytes 131104 | tf_op jit(solution)/shard_map/ppermute | solution.py:326
  20.7 0.2 collective-permute-done.2.refs_0_
  20.9 0.0 copy-start.1
  20.9 1.6 %copy-done.1 = f32[128,4096]{1,0:T(8,128)S(1)} copy-done((f32[128,4096]{1,0:T(8,128)S(1)}, f32[128,4096]{1,0:T(8,128)}, u32[]{:S(2)}) %copy-start.1) | copy-done | bytes 2097176
  22.5 0.0 copy-start.5
  22.5 1.6 %copy-done.5 = f32[128,4096]{1,0:T(8,128)S(1)} copy-done((f32[128,4096]{1,0:T(8,128)S(1)}, f32[128,4096]{1,0:T(8,128)}, u32[]{:S(2)}) %copy-start.5) | copy-done | bytes 2097176
  24.1 0.0 copy-start.7
  24.1 0.9 %copy-done.7 = f32[128,512]{1,0:T(8,128)S(1)} copy-done((f32[128,512]{1,0:T(8,128)S(1)}, f32[128,512]{1,0:T(8,128)}, u32[]{:S(2)}) %copy-start.7) | copy-done | bytes 262168
  25.0 0.0 copy-start.8
  25.0 0.7 %shard_map.48 = (bf16[256,512]{1,0:T(8,128)(2,1)S(1)}, f32[128,4096]{1,0:T(8,128)S(1)}, f32[128,4096]{1,0:T(8,128)S(1)}, f32[128,4096]{1,0:T(8,128)S(1)}) custom-call(s32[1]{0:T(128)} %get-tuple-element.19.needed_ref, f32[128,512]{1,0:T(8,128)S(1)} %copy-done.7, ...), custom_call_target="tpu_custom_call", output_to_operand_aliasing={{0}: (5, {}), {1}: (6, {}), {2}: (7, {}), {3}: (8, {})} | custom-call | flops 4194304 | bytes 524288 | tf_op jit(solution)/shard_map/pallas_call | solution.py:292
  25.8 0.0 copy-start.2
  25.8 1.3 %copy-done.2 = f32[128,4096]{1,0:T(8,128)} copy-done((f32[128,4096]{1,0:T(8,128)}, f32[128,4096]{1,0:T(8,128)S(1)}, u32[]{:S(2)}) %copy-start.2) | copy-done | bytes 2097176
  27.1 0.0 collective-permute-done.refs_1_
  27.1 4.1 %collective-permute-start.4 = (bf16[256,512]{1,0:T(8,128)(2,1)S(1)}, bf16[256,512]{1,0:T(8,128)(2,1)S(1)}, u32[]{:S(2)}, u32[]{:S(2)}) collective-permute-start(bf16[256,512]{1,0:T(8,128)(2,1)S(1)} %broadcast_select_fusion), channel_id=1, source_target_pairs={{0,1},{1,0},{2,3},{3,2},{4,5},{5,4},{6,7},{7,6},{8,9},{9,8},{10,11... | collective-permute-start | bytes 786440 | tf_op jit(solution)/shard_map/ppermute | solution.py:326
  31.3 1.2 %collective-permute-done.4.refs_0_ = bf16[256,512]{1,0:T(8,128)(2,1)S(1)} collective-permute-done((bf16[256,512]{1,0:T(8,128)(2,1)S(1)}, bf16[256,512]{1,0:T(8,128)(2,1)S(1)}, u32[]{:S(2)}, u32[]{:S(2)}) %collective-permute-start.4) | collective-permute-done | bytes 262176 | tf_op jit(solution)/shard_map/ppermute | solution.py:326
  32.4 0.0 copy-done.8
  32.4 0.0 copy-start.3
  32.4 1.6 %copy-done.3 = f32[128,4096]{1,0:T(8,128)S(1)} copy-done((f32[128,4096]{1,0:T(8,128)S(1)}, f32[128,4096]{1,0:T(8,128)}, u32[]{:S(2)}) %copy-start.3) | copy-done | bytes 2097176
  34.0 2.9 %shard_map.49 = bf16[128,4096]{1,0:T(8,128)(2,1)} custom-call(s32[1]{0:T(128)} %get-tuple-element.19.needed_ref, f32[128,512]{1,0:T(8,128)S(1)} %copy-done.8, bf16[128,4096]{1,0:T(8,128)(2,1)S(1)} %get-tuple-element.21.q_ref, bf16[256,512]{1,0:T(8,128)(2,1)S(1)} %collective-permute-done.4.refs_0_, bf16[256,512]{1,0:T(8,128)(2,1)} %collective-permute-done.refs_1_, ...), custom_call_target="tpu_custom_call" | custom-call | flops 4194304 | bytes 524288 | tf_op jit(solution)/shard_map/pallas_call | solution.py:292
  (1 shorter events, 0.0 us)
Async XLA Ops:
  1.9 16.3 %collective-permute-start.1 = (bf16[256,512]{1,0:T(8,128)(2,1)}, bf16[256,512]{1,0:T(8,128)(2,1)S(1)}, u32[]{:S(2)}, u32[]{:S(2)}) collective-permute-start(bf16[256,512]{1,0:T(8,128)(2,1)} %get-tuple-element.23), channel_id=1, source_target_pairs={{0,2},{1,3},{2,4},{3,5},{4,6},{5,7},{6,8},{7,9},{8,10},{9,11},{10,... | collective-permute-start | bytes 786440 | tf_op jit(solution)/shard_map/ppermute | solution.py:312
  10.8 1.3 %copy-start = (f32[128,4096]{1,0:T(8,128)}, f32[128,4096]{1,0:T(8,128)S(1)}, u32[]{:S(2)}) copy-start(f32[128,4096]{1,0:T(8,128)S(1)} %get-tuple-element.25.refs_4_) | copy-start | bytes 6291460
  12.1 1.3 %copy-start.4 = (f32[128,4096]{1,0:T(8,128)}, f32[128,4096]{1,0:T(8,128)S(1)}, u32[]{:S(2)}) copy-start(f32[128,4096]{1,0:T(8,128)S(1)} %get-tuple-element.26.refs_5_) | copy-start | bytes 6291460
  13.5 0.7 %copy-start.6 = (f32[128,512]{1,0:T(8,128)}, f32[128,512]{1,0:T(8,128)S(1)}, u32[]{:S(2)}) copy-start(f32[128,512]{1,0:T(8,128)S(1)} %get-tuple-element.20.bias_ref) | copy-start | bytes 786436
  14.2 13.0 %collective-permute-start = (bf16[256,512]{1,0:T(8,128)(2,1)}, bf16[256,512]{1,0:T(8,128)(2,1)}, u32[]{:S(2)}, u32[]{:S(2)}) collective-permute-start(bf16[256,512]{1,0:T(8,128)(2,1)} %get-tuple-element.22), channel_id=1, source_target_pairs={{0,4},{1,5},{2,6},{3,7},{4,8},{5,9},{6,10},{7,11},{8,12},{9,13},{1... | collective-permute-start | bytes 786440 | tf_op jit(solution)/shard_map/ppermute | solution.py:312
  19.3 1.4 %collective-permute-start.3 = (bf16[128,512]{1,0:T(8,128)(2,1)S(1)}, bf16[128,512]{1,0:T(8,128)(2,1)S(1)}, u32[]{:S(2)}, u32[]{:S(2)}) collective-permute-start(bf16[128,512]{1,0:T(8,128)(2,1)S(1)} %get-tuple-element.31), channel_id=1, source_target_pairs={{0,1},{1,0},{2,3},{3,2},{4,5},{5,4},{6,7},{7,6},{8,9},{9,8},{10,11... | collective-permute-start | bytes 393224 | tf_op jit(solution)/shard_map/ppermute | solution.py:326
  19.3 1.5 %collective-permute-start.2 = (bf16[128,512]{1,0:T(8,128)(2,1)S(1)}, bf16[128,512]{1,0:T(8,128)(2,1)S(1)}, u32[]{:S(2)}, u32[]{:S(2)}) collective-permute-start(bf16[128,512]{1,0:T(8,128)(2,1)S(1)} %get-tuple-element.32), channel_id=1, source_target_pairs={{0,1},{1,0},{2,3},{3,2},{4,5},{5,4},{6,7},{7,6},{8,9},{9,8},{10,11... | collective-permute-start | bytes 393224 | tf_op jit(solution)/shard_map/ppermute | solution.py:326
  20.9 1.6 %copy-start.1 = (f32[128,4096]{1,0:T(8,128)S(1)}, f32[128,4096]{1,0:T(8,128)}, u32[]{:S(2)}) copy-start(f32[128,4096]{1,0:T(8,128)} %copy-done) | copy-start | bytes 6291460
  22.5 1.6 %copy-start.5 = (f32[128,4096]{1,0:T(8,128)S(1)}, f32[128,4096]{1,0:T(8,128)}, u32[]{:S(2)}) copy-start(f32[128,4096]{1,0:T(8,128)} %copy-done.4) | copy-start | bytes 6291460
  24.1 0.9 %copy-start.7 = (f32[128,512]{1,0:T(8,128)S(1)}, f32[128,512]{1,0:T(8,128)}, u32[]{:S(2)}) copy-start(f32[128,512]{1,0:T(8,128)} %copy-done.6) | copy-start | bytes 786436
  25.0 7.4 %copy-start.8 = (f32[128,512]{1,0:T(8,128)S(1)}, f32[128,512]{1,0:T(8,128)}, u32[]{:S(2)}) copy-start(f32[128,512]{1,0:T(8,128)} %copy-done.6) | copy-start | bytes 786436
  25.8 1.3 %copy-start.2 = (f32[128,4096]{1,0:T(8,128)}, f32[128,4096]{1,0:T(8,128)S(1)}, u32[]{:S(2)}) copy-start(f32[128,4096]{1,0:T(8,128)S(1)} %get-tuple-element.29.refs_3_) | copy-start | bytes 6291460
  27.1 5.3 %collective-permute-start.4 = (bf16[256,512]{1,0:T(8,128)(2,1)S(1)}, bf16[256,512]{1,0:T(8,128)(2,1)S(1)}, u32[]{:S(2)}, u32[]{:S(2)}) collective-permute-start(bf16[256,512]{1,0:T(8,128)(2,1)S(1)} %broadcast_select_fusion), channel_id=1, source_target_pairs={{0,1},{1,0},{2,3},{3,2},{4,5},{5,4},{6,7},{7,6},{8,9},{9,8},{10,11... | collective-permute-start | bytes 786440 | tf_op jit(solution)/shard_map/ppermute | solution.py:326
  32.4 1.6 %copy-start.3 = (f32[128,4096]{1,0:T(8,128)S(1)}, f32[128,4096]{1,0:T(8,128)}, u32[]{:S(2)}) copy-start(f32[128,4096]{1,0:T(8,128)} %copy-done.2) | copy-start | bytes 6291460
